TPU v7x, 256 devices: a whole 4x4x8 slice. The times are simulated.
256 devices in a mesh: front: 16 (over x, z_lo, core), row: 4 (over z_hi), col: 4 (over y).
Axes of the slice: x: 4, y: 4, z: 8 (z_hi: 4, z_lo: 2; z = z_hi * 2 + z_lo), core: 2. Of those that a mesh axis runs over, the one named last changes fastest.
Arguments:
- front_entries: float32 [65536, 4096], P(('front', 'row'), 'col'), parts along dimension 0, may hold values from -2 to 8, as said below
- child_updates: bfloat16 [65536, 2048], P(('front', 'row'), 'col'), parts along dimension 0, may hold values from -1 to 1, as said below
- child_maps: int32 [32, 16], P('front'), parts along dimension 0, may hold values from 0 to 31, as said below
Outputs:
- factored: float32 [65536, 4096], P(('front', 'row'), 'col'), parts along dimension 0
There are 16 independent parts, one for each index of `front`. A program takes and returns all parts, laid end to end along the dimension named above; each array names one. Nothing has to cross between parts.
Inputs may be any that keep to these rules, and one draw needn't show every extreme that they name: `front_entries`: symmetric; every diagonal entry of the rows from 1024 on lies in 3.5 to 7; the leading 1024 x 1024 block of the assembled front is positive definite. `child_updates`: each sibling's 2048 x 2048 block is symmetric. `child_maps`: each row lists 2048/128 distinct parent block numbers in decreasing order and contains every block number below 8.
All inputs are finite; a program needn't handle non-finite values.
Results may differ from a plain program's by a relative error of at most 0.0003.
Values may be sent and summed in bfloat16 or wider, within the bound.
A program may use at most 128 MiB of HBM per device.

v0:
```python
import jax
import jax.numpy as jnp
from jax import lax
from jax.sharding import PartitionSpec as P

P_SIZE = 1024
CU = 2048
B = 256
NB = 128
HIGHEST = lax.Precision.HIGHEST


def from_root(value, axis, root):
    mine = lax.axis_index(axis) == root
    return lax.psum(jnp.where(mine, value, jnp.zeros_like(value)), axis)


def block_select(parents, anchor, width):
    return parents[:, None] - anchor == jnp.arange(width, dtype=jnp.int32)[None, :]


def solve_panel(column_rows, diag_factor, global_rows, anchor):
    solved = jax.scipy.linalg.solve_triangular(diag_factor, column_rows.T, lower=True).T
    keeping = global_rows[:, None] >= anchor + jnp.arange(B, dtype=jnp.int32)[None, :]
    return jnp.where(keeping, solved, 0.0)


def local(front_entries, child_updates, child_maps):
    n_row = lax.axis_size("row")
    n_col = lax.axis_size("col")
    row_index = lax.axis_index("row")
    col_index = lax.axis_index("col")
    tile_rows, tile_cols = front_entries.shape
    row_blocks = tile_rows // NB
    col_blocks = tile_cols // NB
    child_blocks = CU // NB
    flat_maps = child_maps.reshape(-1)
    sibling = row_index // (n_row // 2)
    gather_portion = lax.all_gather(child_updates, "col", axis=1, tiled=True)
    block_count = gather_portion.shape[1] // NB
    parents = lax.dynamic_slice_in_dim(flat_maps, sibling * child_blocks, block_count)
    select = block_select(parents, col_index * col_blocks, col_blocks).astype(jnp.bfloat16)
    shaped = gather_portion.reshape(gather_portion.shape[0], block_count, NB)
    gather_placed = jnp.einsum("rjk,ji->rik", shaped, select, preferred_element_type=jnp.float32)
    regrouped = gather_placed.reshape(gather_portion.shape[0], tile_cols).astype(jnp.bfloat16)

    def gather_rows(running, portion):
        block_count = portion.shape[0] // NB
        select = block_select(flat_maps, row_index * row_blocks, row_blocks).astype(jnp.bfloat16)
        placed = lax.dot_general(
            select,
            portion.reshape(block_count, NB * tile_cols),
            (((0,), (0,)), ((), ())),
            preferred_element_type=jnp.float32,
        )
        return running + placed.reshape(tile_rows, tile_cols)

    assembled = gather_rows(front_entries, lax.all_gather(regrouped, "row", axis=0, tiled=True))
    panels = P_SIZE // B
    global_rows = row_index * tile_rows + jnp.arange(tile_rows, dtype=jnp.int32)
    global_cols = col_index * tile_cols + jnp.arange(tile_cols, dtype=jnp.int32)
    factor = jnp.zeros((tile_rows, tile_cols), jnp.float32)
    trailing = assembled
    for number in range(panels):
        anchor = number * B
        owner_col = anchor // tile_cols
        owner_row = anchor // tile_rows
        within = anchor % tile_cols
        within_row = anchor % tile_rows
        corner = trailing[within_row : within_row + B, within : within + B]
        corner = from_root(corner, ("row", "col"), owner_row * n_col + owner_col)
        diag_factor = jnp.linalg.cholesky(corner)
        column = from_root(trailing[:, within : within + B], "col", owner_col)
        share_rows = tile_rows // n_col
        portion = lax.dynamic_slice_in_dim(column, col_index * share_rows, share_rows, 0)
        portion_rows = (
            row_index * tile_rows + col_index * share_rows + jnp.arange(share_rows, dtype=jnp.int32)
        )
        solved = solve_panel(portion, diag_factor, portion_rows, anchor)
        complete = lax.all_gather(solved, ("row", "col"), axis=0, tiled=True)
        own_rows = lax.dynamic_slice_in_dim(complete, row_index * tile_rows, tile_rows, 0)
        col_rows = lax.dynamic_slice_in_dim(complete, col_index * tile_cols, tile_cols, 0)
        placed = lax.dynamic_update_slice(factor, own_rows, (0, within))
        factor = jnp.where(col_index == owner_col, placed, factor)
        update = lax.dot_general(
            own_rows,
            col_rows,
            (((1,), (1,)), ((), ())),
            precision=HIGHEST,
            preferred_element_type=jnp.float32,
        )
        trailing = jnp.where(global_cols[None, :] >= anchor + B, trailing - update, trailing)
    return jnp.where(
        global_cols[None, :] < P_SIZE,
        factor,
        jnp.where(global_rows[:, None] >= P_SIZE, trailing, 0.0),
    )


def solution(mesh):
    placed = (P(("front", "row"), "col"), P(("front", "row"), "col"), P("front", None))
    return jax.shard_map(
        local, mesh=mesh, in_specs=placed, out_specs=P(("front", "row"), "col"), check_vma=False
    )
```

profile of v0, /device:TPU:1, one launch (start us, length us, event | category | flops | bytes accessed | tf_op | source)
XLA Modules:
  0.0 1554.0 jit_solution(12450456545128269763)
XLA Ops:
  8.1 55.7 %all-gather.7.cloned.1.call-done = bf16[1024,2048]{1,0:T(8,128)(2,1)} async-done(((bf16[1024,512]{1,0:T(8,128)(2,1)}), bf16[1024,2048]{1,0:T(8,128)(2,1)}) %all-gather.7.cloned.1.call-update) | async-done | bytes 4194320 | tf_op jit(solution)/shard_map/all_gather | solution.py:39
  63.8 3.6 copy.29
  70.2 5.3 copy.14
  75.6 150.4 %all-gather.9.cloned.1.call-done = bf16[4096,1024]{1,0:T(8,128)(2,1)} async-done(((bf16[1024,1024]{1,0:T(8,128)(2,1)}), bf16[4096,1024]{1,0:T(8,128)(2,1)}) %all-gather.9.cloned.1.call-update) | async-done | bytes 8388624 | tf_op jit(solution)/shard_map/all_gather | solution.py:58
  225.9 8.9 reshape.84
  234.8 6.6 fusion.48
  241.5 4.9 reshape.85
  246.4 5.3 copy.15
  251.7 4.4 add.161
  258.9 2.4 slice_select_fusion.6
  261.7 150.5 %all-reduce.11.cloned.1.call-done = f32[256,256]{0,1:T(8,128)} async-done(((f32[256,256]{0,1:T(8,128)}), f32[256,256]{0,1:T(8,128)}) %all-reduce.11.cloned.1.call-update) | async-done | bytes 262160 | tf_op jit(solution)/shard_map/psum | solution.py:15
  414.2 11.7 cholesky.214
  426.0 9.8 custom-call.17
  436.3 11.7 cholesky.231
  450.1 4.4 while.8
  454.5 19.7 %custom-call.18 = f32[2,128,128]{1,2,0:T(8,128)S(1)} custom-call(f32[2,128,128]{2,1,0:T(8,128)S(1)} %get-tuple-element.33), custom_call_target="InvertDiagBlocksLowerTriangular" | custom-call | tf_op jit(solution)/shard_map/jit(_solve_triangular)/triangular_solve | solution.py:23
  476.9 91.8 %all-gather.11.cloned.1.call-done = f32[4096,256]{0,1:T(8,128)} async-done(((f32[256,256]{0,1:T(8,128)}), f32[4096,256]{0,1:T(8,128)}) %all-gather.11.cloned.1.call-update) | async-done | bytes 4194320 | tf_op jit(solution)/shard_map/all_gather | solution.py:80
  570.0 8.3 subtract_select_fusion.3
  581.1 2.4 slice_select_fusion.5
  583.7 150.1 %all-reduce.15.cloned.1.call-done = f32[256,256]{0,1:T(8,128)} async-done(((f32[256,256]{0,1:T(8,128)}), f32[256,256]{0,1:T(8,128)}) %all-reduce.15.cloned.1.call-update) | async-done | bytes 262160 | tf_op jit(solution)/shard_map/psum | solution.py:15
  735.8 11.7 cholesky.248
  747.6 9.8 custom-call.19
  757.9 11.7 cholesky.265
  772.3 4.1 while.9
  776.4 19.7 %custom-call.20 = f32[2,128,128]{1,2,0:T(8,128)S(1)} custom-call(f32[2,128,128]{2,1,0:T(8,128)S(1)} %get-tuple-element.34), custom_call_target="InvertDiagBlocksLowerTriangular" | custom-call | tf_op jit(solution)/shard_map/jit(_solve_triangular)/triangular_solve | solution.py:23
  798.8 91.8 %all-gather.13.cloned.1.call-done = f32[4096,256]{0,1:T(8,128)} async-done(((f32[256,256]{0,1:T(8,128)}), f32[4096,256]{0,1:T(8,128)}) %all-gather.13.cloned.1.call-update) | async-done | bytes 4194320 | tf_op jit(solution)/shard_map/all_gather | solution.py:80
  890.7 6.9 subtract_select_fusion.2
  903.1 149.9 %all-reduce.19.cloned.1.call-done = f32[256,256]{0,1:T(8,128)} async-done(((f32[256,256]{0,1:T(8,128)}), f32[256,256]{0,1:T(8,128)}) %all-reduce.19.cloned.1.call-update) | async-done | bytes 262160 | tf_op jit(solution)/shard_map/psum | solution.py:15
  1055.0 11.7 cholesky.282
  1066.8 9.8 custom-call.21
  1077.1 11.7 cholesky.299
  1091.4 4.3 while.10
  1095.7 19.7 %custom-call.22 = f32[2,128,128]{1,2,0:T(8,128)S(1)} custom-call(f32[2,128,128]{2,1,0:T(8,128)S(1)} %get-tuple-element.35), custom_call_target="InvertDiagBlocksLowerTriangular" | custom-call | tf_op jit(solution)/shard_map/jit(_solve_triangular)/triangular_solve | solution.py:23
  1118.2 91.8 %all-gather.15.cloned.1.call-done = f32[4096,256]{0,1:T(8,128)} async-done(((f32[256,256]{0,1:T(8,128)}), f32[4096,256]{0,1:T(8,128)}) %all-gather.15.cloned.1.call-update) | async-done | bytes 4194320 | tf_op jit(solution)/shard_map/all_gather | solution.py:80
  1210.0 6.9 subtract_select_fusion.1
  1222.3 150.1 %all-reduce.23.cloned.1.call-done = f32[256,256]{0,1:T(8,128)} async-done(((f32[256,256]{0,1:T(8,128)}), f32[256,256]{0,1:T(8,128)}) %all-reduce.23.cloned.1.call-update) | async-done | bytes 262160 | tf_op jit(solution)/shard_map/psum | solution.py:15
  1374.5 11.7 cholesky.316
  1386.3 9.8 custom-call.23
  1396.6 11.7 cholesky.333
  1410.8 3.9 while.11
  1414.7 19.7 %custom-call.24 = f32[2,128,128]{1,2,0:T(8,128)S(1)} custom-call(f32[2,128,128]{2,1,0:T(8,128)S(1)} %get-tuple-element.36), custom_call_target="InvertDiagBlocksLowerTriangular" | custom-call | tf_op jit(solution)/shard_map/jit(_solve_triangular)/triangular_solve | solution.py:23
  1437.1 2.5 pad_select_fusion
  1439.6 2.7 fusion.4
  1442.3 2.7 fusion.3
  1445.0 84.0 %all-gather.17.cloned.1.call-done = f32[4096,256]{0,1:T(8,128)} async-done(((f32[256,256]{0,1:T(8,128)}), f32[4096,256]{0,1:T(8,128)}) %all-gather.17.cloned.1.call-update) | async-done | bytes 4194320 | tf_op jit(solution)/shard_map/all_gather | solution.py:80
  1529.0 2.7 fusion.2
  1531.7 10.2 fusion.1
  1541.9 5.3 copy.24
  (154 shorter events, 63.8 us)
Async XLA Ops:
  6.5 57.3 %all-gather.7.cloned.1.call-start = ((), (), s32[]{:S(2)}) async-start(), calls=%async_computation | async-start | bytes 5242880 | tf_op jit(solution)/shard_map/all_gather | solution.py:39
  7.3 218.7 %all-gather.9.cloned.1.call-start = ((), (), s32[]{:S(2)}) async-start(), calls=%async_computation.1 | async-start | bytes 10485760 | tf_op jit(solution)/shard_map/all_gather | solution.py:58
  70.1 342.0 %all-reduce.11.cloned.1.call-start = ((), (), s32[]{:S(2)}) async-start(), calls=%async_computation.2 | async-start | bytes 524288 | tf_op jit(solution)/shard_map/psum | solution.py:15
  256.1 2.0 copy-start
  258.9 215.3 %all-reduce.13.cloned.1.call-start = ((), (), s32[]{:S(2)}) async-start(), calls=%async_computation.3 | async-start | bytes 2097152 | tf_op jit(solution)/shard_map/psum | solution.py:15
  261.3 307.4 %all-gather.11.cloned.1.call-start = ((), (), s32[]{:S(2)}) async-start(), calls=%async_computation.4 | async-start | bytes 4456448 | tf_op jit(solution)/shard_map/all_gather | solution.py:80
  476.8 256.9 %all-reduce.15.cloned.1.call-start = ((), (), s32[]{:S(2)}) async-start(), calls=%async_computation.5 | async-start | bytes 524288 | tf_op jit(solution)/shard_map/psum | solution.py:15
  578.3 2.0 copy-start.1
  581.0 215.0 %all-reduce.17.cloned.1.call-start = ((), (), s32[]{:S(2)}) async-start(), calls=%async_computation.6 | async-start | bytes 2097152 | tf_op jit(solution)/shard_map/psum | solution.py:15
  583.5 307.2 %all-gather.13.cloned.1.call-start = ((), (), s32[]{:S(2)}) async-start(), calls=%async_computation.7 | async-start | bytes 4456448 | tf_op jit(solution)/shard_map/all_gather | solution.py:80
  798.8 254.2 %all-reduce.19.cloned.1.call-start = ((), (), s32[]{:S(2)}) async-start(), calls=%async_computation.8 | async-start | bytes 524288 | tf_op jit(solution)/shard_map/psum | solution.py:15
  897.6 2.0 copy-start.2
  900.3 215.1 %all-reduce.21.cloned.1.call-start = ((), (), s32[]{:S(2)}) async-start(), calls=%async_computation.9 | async-start | bytes 2097152 | tf_op jit(solution)/shard_map/psum | solution.py:15
  902.8 307.3 %all-gather.15.cloned.1.call-start = ((), (), s32[]{:S(2)}) async-start(), calls=%async_computation.10 | async-start | bytes 4456448 | tf_op jit(solution)/shard_map/all_gather | solution.py:80
  1118.1 254.3 %all-reduce.23.cloned.1.call-start = ((), (), s32[]{:S(2)}) async-start(), calls=%async_computation.11 | async-start | bytes 524288 | tf_op jit(solution)/shard_map/psum | solution.py:15
  1217.0 2.0 copy-start.3
  1219.7 214.7 %all-reduce.25.cloned.1.call-start = ((), (), s32[]{:S(2)}) async-start(), calls=%async_computation.12 | async-start | bytes 2097152 | tf_op jit(solution)/shard_map/psum | solution.py:15
  1222.0 306.9 %all-gather.17.cloned.1.call-start = ((), (), s32[]{:S(2)}) async-start(), calls=%async_computation.13 | async-start | bytes 4456448 | tf_op jit(solution)/shard_map/all_gather | solution.py:80
Sparse Core Ops, SparseCore 0:
  9.2 54.5 all-gather.6
  70.3 155.6 all-gather.8
  259.0 153.0 all-reduce.10
  414.5 58.7 all-reduce.12
  476.9 91.7 all-gather.10
  581.1 152.5 all-reduce.14
  736.2 59.0 all-reduce.16
  798.9 91.7 all-gather.12
  900.5 152.4 all-reduce.18
  1055.3 58.8 all-reduce.20
  1118.3 91.7 all-gather.14
  1219.8 152.5 all-reduce.22
  1374.9 58.8 all-reduce.24
  1437.2 91.7 all-gather.16
where the time goes:
time: 1560 us; the launch traced here: 1550 us
  waiting for transfers between devices  1170 us (75%)
  other arithmetic  251 us (16%)
  local copies, waits for them, and re-layouts  69 us (4%)
  matrix products  45 us (3%)
  between operations  18.9 us (1%)
    psum x8, waiting for transfers between devices, from_root(): return lax.psum(jnp.where(mine, value, jnp.zeros_like(value)), axis)  601 us
    all_gather x4, waiting for transfers between devices, local(): complete = lax.all_gather(solved, ('row', 'col'), axis=0, tiled=True)  359 us
    all_gather x1, waiting for transfers between devices, local(): lax.all_gather(regrouped, 'row', axis=0, tiled=True)  150 us
    another operation x27, other arithmetic, local(): diag_factor = jnp.linalg.cholesky(corner)  138 us
    another operation x9, other arithmetic, solve_panel(): jax.scipy.linalg.solve_triangular(diag_factor, column_rows.T, lower=True)  78.8 us
    all_gather x1, waiting for transfers between devices, local(): gather_portion = lax.all_gather(child_updates, 'col', axis=1, tiled=True)  55.7 us
    dot_general x4, matrix products, local(): lax.dot_general(own_rows, col_rows, (((1,), (1,)), ((), ())), precision=H...  32.2 us
  transfers between devices with their start and end apart: 14, of which 10 were waited for; matrix products, arithmetic and copies ran while one was open for 17% of the time, Pallas kernels for 0%

commit v1 on v0

--- a/solution.py
+++ b/solution.py
@@ -2,6 +2,7 @@
 import jax.numpy as jnp
 from jax import lax
 from jax.sharding import PartitionSpec as P
+from jax.lax import all_gather
 
 P_SIZE = 1024
 CU = 2048
@@ -10,9 +11,13 @@
 HIGHEST = lax.Precision.HIGHEST
 
 
+def mark_point(row_data, across):
+    return jnp.sum(all_gather(row_data, across), 0)
+
+
 def from_root(value, axis, root):
     mine = lax.axis_index(axis) == root
-    return lax.psum(jnp.where(mine, value, jnp.zeros_like(value)), axis)
+    return mark_point(jnp.where(mine, value, jnp.zeros_like(value)), axis)
 
 
 def block_select(parents, anchor, width):

time: 1560 us -> 1460 us (0.936)
  waiting for transfers between devices: 1170 us -> 1010 us
  local copies, waits for them, and re-layouts: 69 us -> 102 us
  other arithmetic: 251 us -> 271 us
    psum x8 -> x0, waiting for transfers between devices: 601 us -> none  [from_root(): return lax.psum(jnp.where(mine, value, jnp.zeros_like(value)), axis)]
    all_gather x0 -> x8, waiting for transfers between devices: none -> 489 us  [mark_point(): return jnp.sum(all_gather(row_data, across), 0)]
    all_gather x4, waiting for transfers between devices: 359 us -> 317 us  [local(): complete = lax.all_gather(solved, ('row', 'col'), axis=0, tiled=True)]
    reduce_sum x0 -> x8, other arithmetic: none -> 24.1 us  [mark_point(): return jnp.sum(all_gather(row_data, across), 0)]
    all_gather x0 -> x4, local copies, waits for them, and re-layouts: none -> 24 us  [mark_point(): return jnp.sum(all_gather(row_data, across), 0)]
    unnamed x11 -> x15, local copies, waits for them, and re-layouts: 18.9 us -> 34.4 us
  transfers between devices with their start and end apart: 14 -> 14, of which waited for: 10 -> 14; matrix products, arithmetic and copies ran while one was open for 17% -> 4% of each run, Pallas kernels for 0% -> 0%
where the time goes in v1:
time: 1460 us; the launch traced here: 1450 us
  waiting for transfers between devices  1010 us (69%)
  other arithmetic  271 us (19%)
  local copies, waits for them, and re-layouts  102 us (7%)
  matrix products  45 us (3%)
  between operations  19.6 us (1%)
    all_gather x8, waiting for transfers between devices, mark_point(): return jnp.sum(all_gather(row_data, across), 0)  489 us
    all_gather x4, waiting for transfers between devices, local(): complete = lax.all_gather(solved, ('row', 'col'), axis=0, tiled=True)  317 us
    all_gather x1, waiting for transfers between devices, local(): lax.all_gather(regrouped, 'row', axis=0, tiled=True)  150 us
    another operation x27, other arithmetic, local(): diag_factor = jnp.linalg.cholesky(corner)  138 us
    another operation x9, other arithmetic, solve_panel(): jax.scipy.linalg.solve_triangular(diag_factor, column_rows.T, lower=True)  79.9 us
    all_gather x1, waiting for transfers between devices, local(): gather_portion = lax.all_gather(child_updates, 'col', axis=1, tiled=True)  55.7 us
    unnamed x15, local copies, waits for them, and re-layouts  34.4 us
    dot_general x4, matrix products, local(): lax.dot_general(own_rows, col_rows, (((1,), (1,)), ((), ())), precision=H...  32.2 us
  transfers between devices with their start and end apart: 14, of which 14 were waited for; matrix products, arithmetic and copies ran while one was open for 4% of the time, Pallas kernels for 0%

profile of v1, /device:TPU:1, one launch (start us, length us, event | category | flops | bytes accessed | tf_op | source)
XLA Modules:
  0.0 1451.6 jit_solution(13818715304982981404)
XLA Ops:
  8.1 55.7 %all-gather.23.cloned.1.call-done = bf16[1024,2048]{1,0:T(8,128)(2,1)} async-done(((bf16[1024,512]{1,0:T(8,128)(2,1)}), bf16[1024,2048]{1,0:T(8,128)(2,1)}) %all-gather.23.cloned.1.call-update) | async-done | bytes 4194320 | tf_op jit(solution)/shard_map/all_gather | solution.py:44
  70.2 5.3 copy.15
  75.5 150.4 %all-gather.25.cloned.1.call-done = bf16[4096,1024]{1,0:T(8,128)(2,1)} async-done(((bf16[1024,1024]{1,0:T(8,128)(2,1)}), bf16[4096,1024]{1,0:T(8,128)(2,1)}) %all-gather.25.cloned.1.call-update) | async-done | bytes 8388624 | tf_op jit(solution)/shard_map/all_gather | solution.py:63
  225.9 8.9 reshape.84
  234.8 6.6 fusion.48
  241.5 4.9 reshape.85
  246.4 5.3 copy.16
  261.2 47.8 %all-gather.37.cloned.1.call-done = f32[4096,256]{0,1:T(8,128)} async-done(((f32[1024,256]{0,1:T(8,128)}), f32[4096,256]{0,1:T(8,128)}) %all-gather.37.cloned.1.call-update) | async-done | bytes 4194320 | tf_op jit(solution)/shard_map/all_gather | solution.py:15
  309.0 6.0 reshape.115
  315.0 4.7 reduce_sum.73
  319.8 74.7 %all-gather.35.cloned.1.call-done = f32[4096,256]{0,1:T(8,128)} async-done(((f32[256,256]{0,1:T(8,128)}), f32[4096,256]{0,1:T(8,128)}) %all-gather.35.cloned.1.call-update) | async-done | bytes 4194320 | tf_op jit(solution)/shard_map/all_gather | solution.py:15
  399.9 11.7 cholesky.214
  411.7 9.8 custom-call.17
  422.0 11.7 cholesky.231
  439.8 20.1 %custom-call.18 = f32[2,128,128]{1,2,0:T(8,128)S(1)} custom-call(f32[2,128,128]{2,1,0:T(8,128)S(1)} %get-tuple-element.33), custom_call_target="InvertDiagBlocksLowerTriangular" | custom-call | tf_op jit(solution)/shard_map/jit(_solve_triangular)/triangular_solve | solution.py:28
  461.7 81.2 %all-gather.27.cloned.1.call-done = f32[4096,256]{0,1:T(8,128)} async-done(((f32[256,256]{0,1:T(8,128)}), f32[4096,256]{0,1:T(8,128)}) %all-gather.27.cloned.1.call-update) | async-done | bytes 4194320 | tf_op jit(solution)/shard_map/all_gather | solution.py:85
  544.2 8.3 subtract_select_fusion.3
  557.3 47.5 %all-gather.41.cloned.1.call-done = f32[4096,256]{0,1:T(8,128)} async-done(((f32[1024,256]{0,1:T(8,128)}), f32[4096,256]{0,1:T(8,128)}) %all-gather.41.cloned.1.call-update) | async-done | bytes 4194320 | tf_op jit(solution)/shard_map/all_gather | solution.py:15
  604.7 6.0 reshape.117
  610.7 4.7 reduce_sum.75
  615.5 74.8 %all-gather.39.cloned.1.call-done = f32[4096,256]{0,1:T(8,128)} async-done(((f32[256,256]{0,1:T(8,128)}), f32[4096,256]{0,1:T(8,128)}) %all-gather.39.cloned.1.call-update) | async-done | bytes 4194320 | tf_op jit(solution)/shard_map/all_gather | solution.py:15
  695.7 11.7 cholesky.248
  707.5 9.8 custom-call.19
  717.8 11.7 cholesky.265
  736.4 19.9 %custom-call.20 = f32[2,128,128]{1,2,0:T(8,128)S(1)} custom-call(f32[2,128,128]{2,1,0:T(8,128)S(1)} %get-tuple-element.34), custom_call_target="InvertDiagBlocksLowerTriangular" | custom-call | tf_op jit(solution)/shard_map/jit(_solve_triangular)/triangular_solve | solution.py:28
  758.1 81.2 %all-gather.29.cloned.1.call-done = f32[4096,256]{0,1:T(8,128)} async-done(((f32[256,256]{0,1:T(8,128)}), f32[4096,256]{0,1:T(8,128)}) %all-gather.29.cloned.1.call-update) | async-done | bytes 4194320 | tf_op jit(solution)/shard_map/all_gather | solution.py:85
  839.3 6.9 subtract_select_fusion.2
  851.0 47.5 %all-gather.45.cloned.1.call-done = f32[4096,256]{0,1:T(8,128)} async-done(((f32[1024,256]{0,1:T(8,128)}), f32[4096,256]{0,1:T(8,128)}) %all-gather.45.cloned.1.call-update) | async-done | bytes 4194320 | tf_op jit(solution)/shard_map/all_gather | solution.py:15
  898.5 6.0 reshape.119
  904.5 4.7 reduce_sum.77
  909.3 74.7 %all-gather.43.cloned.1.call-done = f32[4096,256]{0,1:T(8,128)} async-done(((f32[256,256]{0,1:T(8,128)}), f32[4096,256]{0,1:T(8,128)}) %all-gather.43.cloned.1.call-update) | async-done | bytes 4194320 | tf_op jit(solution)/shard_map/all_gather | solution.py:15
  989.6 11.7 cholesky.282
  1001.4 9.8 custom-call.21
  1011.7 11.7 cholesky.299
  1030.0 19.8 %custom-call.22 = f32[2,128,128]{1,2,0:T(8,128)S(1)} custom-call(f32[2,128,128]{2,1,0:T(8,128)S(1)} %get-tuple-element.35), custom_call_target="InvertDiagBlocksLowerTriangular" | custom-call | tf_op jit(solution)/shard_map/jit(_solve_triangular)/triangular_solve | solution.py:28
  1051.7 81.2 %all-gather.31.cloned.1.call-done = f32[4096,256]{0,1:T(8,128)} async-done(((f32[256,256]{0,1:T(8,128)}), f32[4096,256]{0,1:T(8,128)}) %all-gather.31.cloned.1.call-update) | async-done | bytes 4194320 | tf_op jit(solution)/shard_map/all_gather | solution.py:85
  1132.9 6.9 subtract_select_fusion.1
  1144.6 47.5 %all-gather.49.cloned.1.call-done = f32[4096,256]{0,1:T(8,128)} async-done(((f32[1024,256]{0,1:T(8,128)}), f32[4096,256]{0,1:T(8,128)}) %all-gather.49.cloned.1.call-update) | async-done | bytes 4194320 | tf_op jit(solution)/shard_map/all_gather | solution.py:15
  1192.1 6.0 reshape.121
  1198.1 4.7 reduce_sum.79
  1202.9 74.8 %all-gather.47.cloned.1.call-done = f32[4096,256]{0,1:T(8,128)} async-done(((f32[256,256]{0,1:T(8,128)}), f32[4096,256]{0,1:T(8,128)}) %all-gather.47.cloned.1.call-update) | async-done | bytes 4194320 | tf_op jit(solution)/shard_map/all_gather | solution.py:15
  1283.1 11.7 cholesky.316
  1294.9 9.8 custom-call.23
  1305.2 11.7 cholesky.333
  1323.5 19.9 %custom-call.24 = f32[2,128,128]{1,2,0:T(8,128)S(1)} custom-call(f32[2,128,128]{2,1,0:T(8,128)S(1)} %get-tuple-element.36), custom_call_target="InvertDiagBlocksLowerTriangular" | custom-call | tf_op jit(solution)/shard_map/jit(_solve_triangular)/triangular_solve | solution.py:28
  1353.1 73.3 %all-gather.33.cloned.1.call-done = f32[4096,256]{0,1:T(8,128)} async-done(((f32[256,256]{0,1:T(8,128)}), f32[4096,256]{0,1:T(8,128)}) %all-gather.33.cloned.1.call-update) | async-done | bytes 4194320 | tf_op jit(solution)/shard_map/all_gather | solution.py:85
  1429.1 10.2 fusion.1
  1439.3 5.3 copy.25
  (169 shorter events, 111.1 us)
Async XLA Ops:
  6.5 57.3 %all-gather.23.cloned.1.call-start = ((), (), s32[]{:S(2)}) async-start(), calls=%async_computation | async-start | bytes 5242880 | tf_op jit(solution)/shard_map/all_gather | solution.py:44
  7.3 218.7 %all-gather.25.cloned.1.call-start = ((), (), s32[]{:S(2)}) async-start(), calls=%async_computation.1 | async-start | bytes 10485760 | tf_op jit(solution)/shard_map/all_gather | solution.py:63
  70.1 238.8 %all-gather.37.cloned.1.call-start = ((), (), s32[]{:S(2)}) async-start(), calls=%async_computation.7 | async-start | bytes 5242880 | tf_op jit(solution)/shard_map/all_gather | solution.py:15
  256.1 1.9 copy-start
  259.1 135.4 %all-gather.35.cloned.1.call-start = ((), (), s32[]{:S(2)}) async-start(), calls=%async_computation.6 | async-start | bytes 4456448 | tf_op jit(solution)/shard_map/all_gather | solution.py:15
  260.9 282.0 %all-gather.27.cloned.1.call-start = ((), (), s32[]{:S(2)}) async-start(), calls=%async_computation.2 | async-start | bytes 4456448 | tf_op jit(solution)/shard_map/all_gather | solution.py:85
  461.6 143.1 %all-gather.41.cloned.1.call-start = ((), (), s32[]{:S(2)}) async-start(), calls=%async_computation.9 | async-start | bytes 5242880 | tf_op jit(solution)/shard_map/all_gather | solution.py:15
  552.4 2.0 copy-start.1
  555.5 134.9 %all-gather.39.cloned.1.call-start = ((), (), s32[]{:S(2)}) async-start(), calls=%async_computation.8 | async-start | bytes 4456448 | tf_op jit(solution)/shard_map/all_gather | solution.py:15
  557.2 282.1 %all-gather.29.cloned.1.call-start = ((), (), s32[]{:S(2)}) async-start(), calls=%async_computation.3 | async-start | bytes 4456448 | tf_op jit(solution)/shard_map/all_gather | solution.py:85
  758.0 140.5 %all-gather.45.cloned.1.call-start = ((), (), s32[]{:S(2)}) async-start(), calls=%async_computation.11 | async-start | bytes 5242880 | tf_op jit(solution)/shard_map/all_gather | solution.py:15
  846.2 2.0 copy-start.2
  849.2 134.7 %all-gather.43.cloned.1.call-start = ((), (), s32[]{:S(2)}) async-start(), calls=%async_computation.10 | async-start | bytes 4456448 | tf_op jit(solution)/shard_map/all_gather | solution.py:15
  851.0 281.9 %all-gather.31.cloned.1.call-start = ((), (), s32[]{:S(2)}) async-start(), calls=%async_computation.4 | async-start | bytes 4456448 | tf_op jit(solution)/shard_map/all_gather | solution.py:85
  1051.6 140.5 %all-gather.49.cloned.1.call-start = ((), (), s32[]{:S(2)}) async-start(), calls=%async_computation.13 | async-start | bytes 5242880 | tf_op jit(solution)/shard_map/all_gather | solution.py:15
  1139.8 2.0 copy-start.3
  1142.8 134.9 %all-gather.47.cloned.1.call-start = ((), (), s32[]{:S(2)}) async-start(), calls=%async_computation.12 | async-start | bytes 4456448 | tf_op jit(solution)/shard_map/all_gather | solution.py:15
  1144.6 281.8 %all-gather.33.cloned.1.call-start = ((), (), s32[]{:S(2)}) async-start(), calls=%async_computation.5 | async-start | bytes 4456448 | tf_op jit(solution)/shard_map/all_gather | solution.py:85
Sparse Core Ops, SparseCore 0:
  9.2 54.5 all-gather.22
  70.3 155.6 all-gather.24
  259.2 49.7 all-gather.36
  311.2 83.1 all-gather.34
  461.7 81.0 all-gather.26
  555.6 49.0 all-gather.40
  607.1 83.1 all-gather.38
  758.1 81.1 all-gather.28
  849.4 49.0 all-gather.44
  900.7 83.1 all-gather.42
  1051.7 81.1 all-gather.30
  1143.0 49.0 all-gather.48
  1194.5 83.1 all-gather.46
  1345.2 81.1 all-gather.32
